TPU v7x, 32 devices: a whole 2x2x4 slice. The times are simulated.
32 devices in a mesh: feat: 4 (over y, x), dp: 8 (over z, core).
Axes of the slice: x: 2, y: 2, z: 4, core: 2. Of those that a mesh axis runs over, the one named last changes fastest.
Arguments:
- text_rows: bfloat16 [1024, 8192], P('dp', 'feat'), may hold values from -6 to 6
- q_weight: bfloat16 [8192, 8192], P(None, 'feat'), may hold values from -0.0625 to 0.0625
- features: bfloat16 [8, 1024, 7680], P('dp', None, 'feat'), may hold values from -6 to 6
- kv_weight: bfloat16 [7680, 2048], P('feat'), may hold values from -0.0625 to 0.0625
- q_gain: float32 [128], replicated, may hold values from 0.7 to 2.6
- k_gain: float32 [128], replicated, may hold values from 0.7 to 2.6
- attn_gate: float32 [1], replicated, may hold values from 0.5 to 2
- image_ids: int32 [128, 2], P('dp'), may hold values from 0 to 7, all different within a row; in each aligned block of 16 rows (0 to 15, 16 to 31, ...) at most 8 rows name the same one
- image_slot: int32 [8], replicated, may hold values from 0 to 7, each once
Outputs:
- attended: bfloat16 [1024, 8192], P('dp', 'feat')
Inputs may be any that keep to these rules, and one draw needn't show every extreme that they name: `image_ids`: each request names two different images; among the requests of one index of dp (aligned blocks of 16 requests) no image is named more than 8 times, a bound that some block reaches. Each position once; image i lies at position image_slot[i].
All inputs are finite; a program needn't handle non-finite values.
Results may differ from a plain program's by a relative error of at most 0.009.
The roundings to bfloat16 on the way count: a program that leaves them out, or rounds other values in their place, can miss the bound.
Values may be sent and summed in bfloat16 or wider, within the bound.
A program may use at most 128 MiB of HBM per device.

v0:
```python
import jax
import jax.numpy as jnp
from jax import lax
from jax.sharding import PartitionSpec as P

epsilon = 1e-05


def head_norm(values, gain_vector):
    return (
        values
        * lax.rsqrt(jnp.mean(values * values, axis=-1, keepdims=True) + epsilon)
        * gain_vector
    )


def attend(queries, keyval, weights):
    head_width = queries.shape[-1]
    scores = jnp.einsum(
        "rhgd,hnd->rhgn", queries, keyval[..., :head_width], preferred_element_type=jnp.float32
    )
    exponent = jnp.exp(scores)
    exponent = exponent * weights[:, None, None, None]
    exponent = exponent.astype(jnp.bfloat16)
    denominator = jnp.sum(exponent.astype(jnp.float32), axis=-1)
    numerator = jnp.einsum(
        "rhgn,hnd->rhgd", exponent, keyval[..., head_width:], preferred_element_type=jnp.float32
    )
    return (numerator, denominator)


def per_device(
    text_rows, q_weight, features, kv_weight, q_gain, k_gain, attn_gate, image_ids, image_slot
):
    row_count = text_rows.shape[0]
    requests = image_ids.shape[0]
    text_words = row_count // requests
    head_width = q_gain.shape[0]
    heads_all = kv_weight.shape[1] // (2 * head_width)
    kv_local = heads_all // lax.axis_size("feat")
    group_size = q_weight.shape[1] // (head_width * kv_local)
    weight_block = q_weight
    queries = jnp.dot(
        lax.all_gather(text_rows, "feat", axis=1, tiled=True),
        weight_block,
        preferred_element_type=jnp.float32,
    )
    queries = head_norm(
        queries.reshape(row_count, kv_local, group_size, head_width), q_gain
    ) * head_width ** (-0.5)
    queries = queries.astype(jnp.bfloat16)
    kv_table = kv_weight.reshape(kv_weight.shape[0], heads_all, 2 * head_width)
    vision_rows = features[0]
    weight_block = kv_table
    summed = lax.psum_scatter(
        jnp.einsum("nf,fhc->hnc", vision_rows, weight_block, preferred_element_type=jnp.float32),
        "feat",
        scatter_dimension=0,
        tiled=True,
    )
    normed_keys = head_norm(summed[..., :head_width], k_gain)
    keyval = jnp.concatenate([normed_keys, summed[..., head_width:]], axis=-1).astype(jnp.bfloat16)
    image_count = image_slot.shape[0]
    matches = image_ids[:, :, None] == jnp.arange(image_count, dtype=jnp.int32)[None, None, :]
    owners = jnp.sum(jnp.where(matches, image_slot[None, None, :], 0), axis=-1)
    starting = (
        jnp.zeros((row_count, kv_local, group_size, head_width), jnp.float32),
        jnp.zeros((row_count, kv_local, group_size), jnp.float32),
    )
    shard_piece = lax.all_gather(keyval[None], "dp", axis=0, tiled=True)

    def add_one(position, partial_sums):
        reads_image = jnp.any(owners == position, axis=1)
        weights = jnp.repeat(reads_image.astype(jnp.float32), text_words)
        kv_block = lax.dynamic_index_in_dim(shard_piece, position, 0, keepdims=False)
        numerator, denominator = attend(queries, kv_block, weights)
        return (partial_sums[0] + numerator, partial_sums[1] + denominator)

    numerator, denominator = lax.fori_loop(0, shard_piece.shape[0], add_one, starting)
    result = numerator / denominator[..., None]
    return (jnp.tanh(attn_gate[0]) * result).astype(jnp.bfloat16).reshape(row_count, -1)


def solution(mesh):
    in_specs = (
        P("dp", "feat"),
        P(None, "feat"),
        P("dp", None, "feat"),
        P("feat", None),
        P(),
        P(),
        P(),
        P("dp", None),
        P(),
    )
    out_specs = P("dp", "feat")
    return jax.shard_map(
        per_device, mesh=mesh, in_specs=in_specs, out_specs=out_specs, check_vma=False
    )
```

profile of v0, /device:TPU:0, one launch (start us, length us, event | category | flops | bytes accessed | tf_op | source)
XLA Modules:
  0.0 316.9 jit_solution(3999134961463907192)
XLA Ops:
  6.5 10.7 %copy.49 = bf16[1920,2048]{0,1:T(8,128)(2,1)} copy(bf16[1920,2048]{1,0:T(8,128)(2,1)} %param.14) | data formatting | bytes 15728640 | tf_op jit(solution)/shard_map/reshape | solution.py:52
  17.3 14.3 %fusion.4 = f32[8,1024,256]{1,2,0:T(8,128)} fusion(bf16[1920,8,256]{0,2,1:T(8,128)(2,1)} %bitcast.58, bf16[1,1024,1920]{2,1,0:T(8,128)(2,1)} %param.13), kind=kOutput, calls=%fused_computation.12 | convolution fusion | flops 8053063680 | bytes 20185088 | tf_op jit(solution)/shard_map/nf,fhc->hnc/dot_general | solution.py:56
  31.7 0.7 all-gather.5.cloned.1.call-update
  32.4 88.5 %reduce-scatter.2.cloned.1.call-done = f32[2,1024,256]{1,2,0:T(8,128)} async-done(((f32[8,1024,256]{1,2,0:T(8,128)}), f32[2,1024,256]{1,2,0:T(8,128)}) %reduce-scatter.2.cloned.1.call-update) | async-done | bytes 2097168 | tf_op jit(solution)/shard_map/reduce_scatter | solution.py:55
  120.9 1.3 multiply_reduce_fusion.1
  122.3 1.3 fusion.11
  123.6 1.4 fusion.10
  125.0 1.3 copy.42
  127.2 31.0 %all-gather.5.cloned.1.call-done = bf16[128,8192]{1,0:T(8,128)(2,1)} async-done(((bf16[128,2048]{1,0:T(8,128)(2,1)}), bf16[128,8192]{1,0:T(8,128)(2,1)}) %all-gather.5.cloned.1.call-update) | async-done | bytes 2097168 | tf_op jit(solution)/shard_map/all_gather | solution.py:44
  158.2 14.8 %convolution_bitcast_fusion.1 = f32[16,8,16,128]{3,1,2,0:T(8,128)S(1)} fusion(bf16[128,8192]{1,0:T(8,128)(2,1)} %all-gather.5.cloned.1.call-done, bf16[8192,2048]{1,0:T(8,128)(2,1)} %param.12), kind=kOutput, calls=%fused_computation.13 | convolution fusion | flops 4294967296 | bytes 36700160 | tf_op jit(solution)/shard_map/dot_general | solution.py:43
  173.0 0.2 copy.53
  173.2 0.4 multiply_reduce_fusion
  173.7 0.5 fusion.9
  174.2 67.8 %all-gather.3.cloned.1.call-done = bf16[8,2,1024,256]{3,2,1,0:T(8,128)(2,1)} async-done(((bf16[1,2,1024,256]{3,2,1,0:T(8,128)(2,1)}), bf16[8,2,1024,256]{3,2,1,0:T(8,128)(2,1)}) %all-gather.3.cloned.1.call-update) | async-done | bytes 8388624 | tf_op jit(solution)/shard_map/all_gather | solution.py:70
  242.0 67.2 %while.16 = (s32[]{:T(128)}, f32[128,2,8,128]{0,3,2,1:T(8,128)S(1)}, f32[128,2,8]{0,2,1:T(8,128)S(1)}, bf16[8,2,1024,256]{3,2,1,0:T(8,128)(2,1)}, bf16[128,2,8,1...) while((s32[]{:T(128)}, f32[128,2,8,128]{0,3,2,1:T(8,128)S(1)}, ...), condition=%wide.region_7.8_spmd.clone, body=%wide.region_4.7_spmd.clone.sunk | while | flops 1082656768 | bytes 14190984 | solution.py:79
  242.0 1.3 dynamic-slice_bitcast_fusion.2
  243.4 0.1 mul.127
  243.5 3.6 %convert_reduce_fusion.2 = (f32[128,2,8]{0,2,1:T(8,128)S(1)}, bf16[128,2,8,1024]{0,3,2,1:T(8,128)(2,1)}) fusion(f32[128]{0:T(128)S(1)} %mul.127, bf16[128,2,8,128]{3,0,2,1:T(8,128)(2,1)S(1)} %get-tuple-element.225, bf16[2,1024,256]{2,1,0:T(8,128)(2,1)S(1)} %dynamic-slice_bitcast_fusion.2), kind=kOutput, calls=%fused_computation.clone.1 | convolution fusion | flops 545257472 | bytes 5251584 | tf_op jit(solution)/shard_map/while/body/eval_jaxpr/rhgd,hnd->rhgn/dot_general | solution.py:19
  247.1 3.2 %fusion.22 = f32[128,2,8,128]{0,3,2,1:T(8,128)S(1)} fusion(bf16[128,2,8,1024]{0,3,2,1:T(8,128)(2,1)} %get-tuple-element.203, f32[128,2,8,128]{0,3,2,1:T(8,128)S(1)} %get-tuple-element.214, bf16[2,1024,256]{2,1,0:T(8,128)(2,1)S(1)} %dynamic-slice_bitcast_fusion.2, pred[]{:T(512)S(6)} %compare.3), kind=kOutput, calls=%fused_computation.4.clone.1 | convolution fusion | flops 537395200 | bytes 6815745 | tf_op jit(solution)/shard_map/while/body/eval_jaxpr/rhgn,hnd->rhgd/dot_general | solution.py:26
  250.4 1.3 dynamic-slice_bitcast_fusion.2
  251.8 0.1 mul.127
  251.9 3.6 %convert_reduce_fusion.2 = (f32[128,2,8]{0,2,1:T(8,128)S(1)}, bf16[128,2,8,1024]{0,3,2,1:T(8,128)(2,1)}) fusion(f32[128]{0:T(128)S(1)} %mul.127, bf16[128,2,8,128]{3,0,2,1:T(8,128)(2,1)S(1)} %get-tuple-element.225, bf16[2,1024,256]{2,1,0:T(8,128)(2,1)S(1)} %dynamic-slice_bitcast_fusion.2), kind=kOutput, calls=%fused_computation.clone.1 | convolution fusion | flops 545257472 | bytes 5251584 | tf_op jit(solution)/shard_map/while/body/eval_jaxpr/rhgd,hnd->rhgn/dot_general | solution.py:19
  255.5 3.2 %fusion.22 = f32[128,2,8,128]{0,3,2,1:T(8,128)S(1)} fusion(bf16[128,2,8,1024]{0,3,2,1:T(8,128)(2,1)} %get-tuple-element.203, f32[128,2,8,128]{0,3,2,1:T(8,128)S(1)} %get-tuple-element.214, bf16[2,1024,256]{2,1,0:T(8,128)(2,1)S(1)} %dynamic-slice_bitcast_fusion.2, pred[]{:T(512)S(6)} %compare.3), kind=kOutput, calls=%fused_computation.4.clone.1 | convolution fusion | flops 537395200 | bytes 6815745 | tf_op jit(solution)/shard_map/while/body/eval_jaxpr/rhgn,hnd->rhgd/dot_general | solution.py:26
  258.8 1.3 dynamic-slice_bitcast_fusion.2
  260.2 0.1 mul.127
  260.3 3.6 %convert_reduce_fusion.2 = (f32[128,2,8]{0,2,1:T(8,128)S(1)}, bf16[128,2,8,1024]{0,3,2,1:T(8,128)(2,1)}) fusion(f32[128]{0:T(128)S(1)} %mul.127, bf16[128,2,8,128]{3,0,2,1:T(8,128)(2,1)S(1)} %get-tuple-element.225, bf16[2,1024,256]{2,1,0:T(8,128)(2,1)S(1)} %dynamic-slice_bitcast_fusion.2), kind=kOutput, calls=%fused_computation.clone.1 | convolution fusion | flops 545257472 | bytes 5251584 | tf_op jit(solution)/shard_map/while/body/eval_jaxpr/rhgd,hnd->rhgn/dot_general | solution.py:19
  263.9 3.2 %fusion.22 = f32[128,2,8,128]{0,3,2,1:T(8,128)S(1)} fusion(bf16[128,2,8,1024]{0,3,2,1:T(8,128)(2,1)} %get-tuple-element.203, f32[128,2,8,128]{0,3,2,1:T(8,128)S(1)} %get-tuple-element.214, bf16[2,1024,256]{2,1,0:T(8,128)(2,1)S(1)} %dynamic-slice_bitcast_fusion.2, pred[]{:T(512)S(6)} %compare.3), kind=kOutput, calls=%fused_computation.4.clone.1 | convolution fusion | flops 537395200 | bytes 6815745 | tf_op jit(solution)/shard_map/while/body/eval_jaxpr/rhgn,hnd->rhgd/dot_general | solution.py:26
  267.2 1.3 dynamic-slice_bitcast_fusion.2
  268.6 0.1 mul.127
  268.7 3.6 %convert_reduce_fusion.2 = (f32[128,2,8]{0,2,1:T(8,128)S(1)}, bf16[128,2,8,1024]{0,3,2,1:T(8,128)(2,1)}) fusion(f32[128]{0:T(128)S(1)} %mul.127, bf16[128,2,8,128]{3,0,2,1:T(8,128)(2,1)S(1)} %get-tuple-element.225, bf16[2,1024,256]{2,1,0:T(8,128)(2,1)S(1)} %dynamic-slice_bitcast_fusion.2), kind=kOutput, calls=%fused_computation.clone.1 | convolution fusion | flops 545257472 | bytes 5251584 | tf_op jit(solution)/shard_map/while/body/eval_jaxpr/rhgd,hnd->rhgn/dot_general | solution.py:19
  272.3 3.2 %fusion.22 = f32[128,2,8,128]{0,3,2,1:T(8,128)S(1)} fusion(bf16[128,2,8,1024]{0,3,2,1:T(8,128)(2,1)} %get-tuple-element.203, f32[128,2,8,128]{0,3,2,1:T(8,128)S(1)} %get-tuple-element.214, bf16[2,1024,256]{2,1,0:T(8,128)(2,1)S(1)} %dynamic-slice_bitcast_fusion.2, pred[]{:T(512)S(6)} %compare.3), kind=kOutput, calls=%fused_computation.4.clone.1 | convolution fusion | flops 537395200 | bytes 6815745 | tf_op jit(solution)/shard_map/while/body/eval_jaxpr/rhgn,hnd->rhgd/dot_general | solution.py:26
  275.6 1.3 dynamic-slice_bitcast_fusion.2
  277.0 0.1 mul.127
  277.1 3.6 %convert_reduce_fusion.2 = (f32[128,2,8]{0,2,1:T(8,128)S(1)}, bf16[128,2,8,1024]{0,3,2,1:T(8,128)(2,1)}) fusion(f32[128]{0:T(128)S(1)} %mul.127, bf16[128,2,8,128]{3,0,2,1:T(8,128)(2,1)S(1)} %get-tuple-element.225, bf16[2,1024,256]{2,1,0:T(8,128)(2,1)S(1)} %dynamic-slice_bitcast_fusion.2), kind=kOutput, calls=%fused_computation.clone.1 | convolution fusion | flops 545257472 | bytes 5251584 | tf_op jit(solution)/shard_map/while/body/eval_jaxpr/rhgd,hnd->rhgn/dot_general | solution.py:19
  280.7 3.2 %fusion.22 = f32[128,2,8,128]{0,3,2,1:T(8,128)S(1)} fusion(bf16[128,2,8,1024]{0,3,2,1:T(8,128)(2,1)} %get-tuple-element.203, f32[128,2,8,128]{0,3,2,1:T(8,128)S(1)} %get-tuple-element.214, bf16[2,1024,256]{2,1,0:T(8,128)(2,1)S(1)} %dynamic-slice_bitcast_fusion.2, pred[]{:T(512)S(6)} %compare.3), kind=kOutput, calls=%fused_computation.4.clone.1 | convolution fusion | flops 537395200 | bytes 6815745 | tf_op jit(solution)/shard_map/while/body/eval_jaxpr/rhgn,hnd->rhgd/dot_general | solution.py:26
  284.0 1.3 dynamic-slice_bitcast_fusion.2
  285.4 0.1 mul.127
  285.5 3.6 %convert_reduce_fusion.2 = (f32[128,2,8]{0,2,1:T(8,128)S(1)}, bf16[128,2,8,1024]{0,3,2,1:T(8,128)(2,1)}) fusion(f32[128]{0:T(128)S(1)} %mul.127, bf16[128,2,8,128]{3,0,2,1:T(8,128)(2,1)S(1)} %get-tuple-element.225, bf16[2,1024,256]{2,1,0:T(8,128)(2,1)S(1)} %dynamic-slice_bitcast_fusion.2), kind=kOutput, calls=%fused_computation.clone.1 | convolution fusion | flops 545257472 | bytes 5251584 | tf_op jit(solution)/shard_map/while/body/eval_jaxpr/rhgd,hnd->rhgn/dot_general | solution.py:19
  289.1 3.2 %fusion.22 = f32[128,2,8,128]{0,3,2,1:T(8,128)S(1)} fusion(bf16[128,2,8,1024]{0,3,2,1:T(8,128)(2,1)} %get-tuple-element.203, f32[128,2,8,128]{0,3,2,1:T(8,128)S(1)} %get-tuple-element.214, bf16[2,1024,256]{2,1,0:T(8,128)(2,1)S(1)} %dynamic-slice_bitcast_fusion.2, pred[]{:T(512)S(6)} %compare.3), kind=kOutput, calls=%fused_computation.4.clone.1 | convolution fusion | flops 537395200 | bytes 6815745 | tf_op jit(solution)/shard_map/while/body/eval_jaxpr/rhgn,hnd->rhgd/dot_general | solution.py:26
  292.4 1.3 dynamic-slice_bitcast_fusion.2
  293.8 0.1 mul.127
  293.9 3.6 %convert_reduce_fusion.2 = (f32[128,2,8]{0,2,1:T(8,128)S(1)}, bf16[128,2,8,1024]{0,3,2,1:T(8,128)(2,1)}) fusion(f32[128]{0:T(128)S(1)} %mul.127, bf16[128,2,8,128]{3,0,2,1:T(8,128)(2,1)S(1)} %get-tuple-element.225, bf16[2,1024,256]{2,1,0:T(8,128)(2,1)S(1)} %dynamic-slice_bitcast_fusion.2), kind=kOutput, calls=%fused_computation.clone.1 | convolution fusion | flops 545257472 | bytes 5251584 | tf_op jit(solution)/shard_map/while/body/eval_jaxpr/rhgd,hnd->rhgn/dot_general | solution.py:19
  297.5 3.2 %fusion.22 = f32[128,2,8,128]{0,3,2,1:T(8,128)S(1)} fusion(bf16[128,2,8,1024]{0,3,2,1:T(8,128)(2,1)} %get-tuple-element.203, f32[128,2,8,128]{0,3,2,1:T(8,128)S(1)} %get-tuple-element.214, bf16[2,1024,256]{2,1,0:T(8,128)(2,1)S(1)} %dynamic-slice_bitcast_fusion.2, pred[]{:T(512)S(6)} %compare.3), kind=kOutput, calls=%fused_computation.4.clone.1 | convolution fusion | flops 537395200 | bytes 6815745 | tf_op jit(solution)/shard_map/while/body/eval_jaxpr/rhgn,hnd->rhgd/dot_general | solution.py:26
  300.8 1.3 dynamic-slice_bitcast_fusion.2
  302.3 3.6 %convert_reduce_fusion.2 = (f32[128,2,8]{0,2,1:T(8,128)S(1)}, bf16[128,2,8,1024]{0,3,2,1:T(8,128)(2,1)}) fusion(f32[128]{0:T(128)S(1)} %mul.127, bf16[128,2,8,128]{3,0,2,1:T(8,128)(2,1)S(1)} %get-tuple-element.225, bf16[2,1024,256]{2,1,0:T(8,128)(2,1)S(1)} %dynamic-slice_bitcast_fusion.2), kind=kOutput, calls=%fused_computation.clone.1 | convolution fusion | flops 545257472 | bytes 5251584 | tf_op jit(solution)/shard_map/while/body/eval_jaxpr/rhgd,hnd->rhgn/dot_general | solution.py:19
  305.9 3.2 %fusion.22 = f32[128,2,8,128]{0,3,2,1:T(8,128)S(1)} fusion(bf16[128,2,8,1024]{0,3,2,1:T(8,128)(2,1)} %get-tuple-element.203, f32[128,2,8,128]{0,3,2,1:T(8,128)S(1)} %get-tuple-element.214, bf16[2,1024,256]{2,1,0:T(8,128)(2,1)S(1)} %dynamic-slice_bitcast_fusion.2, pred[]{:T(512)S(6)} %compare.3), kind=kOutput, calls=%fused_computation.4.clone.1 | convolution fusion | flops 537395200 | bytes 6815745 | tf_op jit(solution)/shard_map/while/body/eval_jaxpr/rhgn,hnd->rhgd/dot_general | solution.py:26
  309.2 0.1 multiply_convert_fusion.1
  309.3 1.0 copy.50
  (53 shorter events, 1.3 us)
Async XLA Ops:
  6.5 114.4 %reduce-scatter.2.cloned.1.call-start = ((), (), s32[]{:S(2)}) async-start(), calls=%async_computation.1 | async-start | bytes 10485760 | tf_op jit(solution)/shard_map/reduce_scatter | solution.py:55
  31.6 92.0 %copy-start.1 = (f32[128]{0:T(128)S(1)}, f32[128]{0:T(128)}, u32[]{:S(2)}) copy-start(f32[128]{0:T(128)} %param.16) | copy-start | bytes 1540
  31.6 126.6 %all-gather.5.cloned.1.call-start = ((), (), s32[]{:S(2)}) async-start(), calls=%async_computation.3 | async-start | bytes 2621440 | tf_op jit(solution)/shard_map/all_gather | solution.py:44
  32.4 209.6 %all-gather.3.cloned.1.call-start = ((), (), s32[]{:S(2)}) async-start(), calls=%async_computation.2 | async-start | bytes 9437184 | tf_op jit(solution)/shard_map/all_gather | solution.py:70
  122.2 4.9 %copy-start = (s32[16,2]{0,1:T(2,128)S(1)}, s32[16,2]{0,1:T(2,128)}, u32[]{:S(2)}) copy-start(s32[16,2]{0,1:T(2,128)} %param.18) | copy-start | bytes 388
  122.2 4.9 %copy-start.3 = (s32[8]{0:T(128)S(1)}, s32[8]{0:T(128)}, u32[]{:S(2)}) copy-start(s32[8]{0:T(128)} %param.19) | copy-start | bytes 100
  127.2 46.5 %copy-start.2 = (f32[128]{0:T(128)S(1)}, f32[128]{0:T(128)}, u32[]{:S(2)}) copy-start(f32[128]{0:T(128)} %param.15) | copy-start | bytes 1540
Sparse Core Ops, SparseCore 0:
  31.7 89.0 reduce-scatter.1
  122.9 35.2 all-gather.4
  159.9 82.0 all-gather.2
where the time goes:
time: 318 us; the launch traced here: 317 us
  waiting for transfers between devices  188 us (59%)
  matrix products  84 us (26%)
  local copies, waits for them, and re-layouts  26.3 us (8%)
  between operations  13.9 us (4%)
  other arithmetic  4.23 us (1%)
    reduce_scatter x1, waiting for transfers between devices, per_device(): lax.psum_scatter(jnp.einsum('nf,fhc->hnc', vision_rows, weight_block, pre...  88.5 us
    all_gather x1, waiting for transfers between devices, per_device(): shard_piece = lax.all_gather(keyval[None], 'dp', axis=0, tiled=True)  67.8 us
    all_gather x1, waiting for transfers between devices, per_device(): lax.all_gather(text_rows, 'feat', axis=1, tiled=True)  31 us
    dot_general x8, matrix products, attend(): jnp.einsum('rhgd,hnd->rhgn', queries, keyval[..., :head_width], preferred...  29.1 us
    dot_general x8, matrix products, attend(): jnp.einsum('rhgn,hnd->rhgd', exponent, keyval[..., head_width:], preferre...  25.8 us
    dot_general x1, matrix products, per_device(): jnp.dot(lax.all_gather(text_rows, 'feat', axis=1, tiled=True), weight_blo...  14.8 us
    dot_general x1, matrix products, per_device(): jnp.einsum('nf,fhc->hnc', vision_rows, weight_block, preferred_element_ty...  14.3 us
    reshape x1, local copies, waits for them, and re-layouts, per_device(): kv_table = kv_weight.reshape(kv_weight.shape[0], heads_all, 2 * head_width)  10.7 us
  transfers between devices with their start and end apart: 3, of which 3 were waited for; matrix products, arithmetic and copies ran while one was open for 7% of the time, Pallas kernels for 0%

commit v1 on v0

v1 whole, which is shorter than its diff:
```python
import functools

import jax
import jax.numpy as jnp
from jax import lax
from jax.experimental import pallas as pl
from jax.experimental.pallas import tpu as pltpu
from jax.sharding import PartitionSpec as P

epsilon = 1e-05
MIB = 1024 * 1024
MESH = pl.DeviceIdType.MESH
HALVES = 2
SLOTS = 3
PIECE = 256


def head_norm(values, gain_vector):
    return (
        values
        * lax.rsqrt(jnp.mean(values * values, axis=-1, keepdims=True) + epsilon)
        * gain_vector
    )


def fused_kernel(
    sizes,
    ids_ref, slot_ref, gate_ref, text_ref, features_ref, q_gain_ref, k_gain_ref, q_weight_ref, kv_weight_ref,
    out_ref,
    vision, kv_table, outgoing, incoming, own, text_full, weights, queries, attended,
    vision_sem, table_sem, rs_send, rs_recv, text_send, text_recv, weight_sem, kv_send, kv_recv,
    *keyval,
):
    feat_count, dp_count, head_width, group, kv_local = sizes
    rows = text_ref.shape[0]
    requests = ids_ref.shape[0]
    text_words = rows // requests
    wide = 2 * head_width
    half_rows = vision.shape[1]
    chunks = kv_local * HALVES
    pieces = q_weight_ref.shape[1] // PIECE
    depth = text_ref.shape[1]
    positions = dp_count // 2
    me_feat, me_dp = lax.axis_index("feat"), lax.axis_index("dp")
    position, core = me_dp // 2, me_dp % 2
    sibling = me_dp + 1 - 2 * core

    def load_vision(half):
        return pltpu.make_async_copy(
            features_ref.at[pl.ds(half * half_rows, half_rows), :], vision.at[half], vision_sem.at[half]
        )

    def load_table(f, h):
        start = pl.multiple_of((f * kv_local + h) * wide, wide)
        return pltpu.make_async_copy(
            kv_weight_ref.at[:, pl.ds(start, wide)], kv_table.at[f, h], table_sem.at[f, h]
        )

    def load_weight(j):
        start = pl.multiple_of(j * PIECE, PIECE)
        return pltpu.make_async_copy(
            q_weight_ref.at[:, pl.ds(start, PIECE)], weights.at[j % SLOTS], weight_sem.at[j]
        )

    load_vision(0).start()
    for h in range(kv_local):
        for d in range(1, feat_count + 1):
            load_table((me_feat + d) % feat_count, h).start()
        if h == 0:
            for half in range(1, HALVES):
                load_vision(half).start()
    for j in range(min(SLOTS, pieces)):
        load_weight(j).start()

    barrier = pltpu.get_barrier_semaphore()
    for d in range(1, feat_count):
        pl.semaphore_signal(barrier, inc=1, device_id={"feat": (me_feat + d) % feat_count}, device_id_type=MESH)
    pl.semaphore_signal(barrier, inc=1, device_id={"dp": sibling}, device_id_type=MESH)

    @pl.when(position > 0)
    def _():
        pl.semaphore_signal(barrier, inc=1, device_id={"dp": me_dp - 2}, device_id_type=MESH)

    @pl.when(position < positions - 1)
    def _():
        pl.semaphore_signal(barrier, inc=1, device_id={"dp": me_dp + 2}, device_id_type=MESH)

    inside = (position > 0) & (position < positions - 1)

    @pl.when(inside)
    def _():
        pl.semaphore_wait(barrier, feat_count + 2)

    @pl.when(jnp.logical_not(inside))
    def _():
        pl.semaphore_wait(barrier, feat_count + min(1, positions - 1))

    text_full[me_feat] = text_ref[...]

    def text_copy(d):
        return pltpu.make_async_remote_copy(
            src_ref=text_ref, dst_ref=text_full.at[me_feat], send_sem=text_send.at[d - 1],
            recv_sem=text_recv.at[d - 1], device_id={"feat": (me_feat + d) % feat_count}, device_id_type=MESH,
        )

    def partial_copy(c, d):
        return pltpu.make_async_remote_copy(
            src_ref=outgoing.at[c, d - 1], dst_ref=incoming.at[c, d - 1], send_sem=rs_send.at[c, d - 1],
            recv_sem=rs_recv.at[c, d - 1], device_id={"feat": (me_feat + d) % feat_count}, device_id_type=MESH,
        )

    def share(c, origin, way, target):
        h, half = c // HALVES, c % HALVES
        block = keyval[h].at[origin, pl.ds(half * half_rows, half_rows), :]
        return pltpu.make_async_remote_copy(
            src_ref=block, dst_ref=block, send_sem=kv_send.at[way, c, origin],
            recv_sem=kv_recv.at[c, origin], device_id={"dp": target}, device_id_type=MESH,
        )

    for c in range(chunks):
        h, half = c // HALVES, c % HALVES
        if h == 0:
            load_vision(half).wait()

        def one_peer(d, carry, c=c, h=h, half=half):
            f = (me_feat + d) % feat_count
            if half == 0:
                load_table(f, h).wait()
            outgoing[c, d - 1] = jnp.dot(
                vision[half], kv_table[f, h], preferred_element_type=jnp.float32
            ).astype(jnp.bfloat16)
            partial_copy(c, d).start()
            return carry

        lax.fori_loop(1, feat_count, one_peer, 0)
        if half == 0:
            load_table(me_feat, h).wait()
        own[c] = jnp.dot(vision[half], kv_table[me_feat, h], preferred_element_type=jnp.float32)
        if c == max(0, chunks - 2):
            for d in range(1, feat_count):
                text_copy(d).start()

    def finish_own(c):
        h, half = c // HALVES, c % HALVES
        summed = own[c]
        for d in range(1, feat_count):
            partial_copy(c, d).wait_recv()
            summed = summed + incoming[c, d - 1].astype(jnp.float32)
        normed_keys = head_norm(summed[:, :head_width], k_gain_ref[...])
        block = jnp.concatenate([normed_keys, summed[:, head_width:]], axis=-1).astype(jnp.bfloat16)
        keyval[h][me_dp, half * half_rows : (half + 1) * half_rows, :] = block

        @pl.when(position > 0)
        def _():
            share(c, me_dp, 0, me_dp - 2).start()

        @pl.when(position < positions - 1)
        def _():
            share(c, me_dp, 1, me_dp + 2).start()

        share(c, me_dp, 2, sibling).start()

    def pass_on(c, distance):
        @pl.when(position >= distance)
        def _():
            origin = me_dp - 2 * distance
            share(c, origin, 1, sibling).wait_recv()

            @pl.when(position < positions - 1)
            def _():
                share(c, origin, 1, me_dp + 2).start()

            share(c, origin, 2, sibling).start()

        @pl.when(position + distance < positions)
        def _():
            origin = me_dp + 2 * distance
            share(c, origin, 0, sibling).wait_recv()

            @pl.when(position > 0)
            def _():
                share(c, origin, 0, me_dp - 2).start()

            share(c, origin, 2, sibling).start()

    def project(j, carry):
        load_weight(j).wait()
        total = jnp.zeros((rows, PIECE), jnp.float32)
        for f in range(feat_count):
            total += jnp.dot(
                text_full[f],
                weights[j % SLOTS, f * depth : (f + 1) * depth, :],
                preferred_element_type=jnp.float32,
            )
        for part in range(PIECE // head_width):
            normed = head_norm(total[:, part * head_width : (part + 1) * head_width], q_gain_ref[...])
            normed = (normed * head_width ** (-0.5)).astype(jnp.bfloat16)
            start = pl.multiple_of(j * PIECE + part * head_width, head_width)
            queries[:, pl.ds(start, head_width)] = normed.astype(jnp.float32)

        @pl.when(j + SLOTS < pieces)
        def _():
            load_weight(j + SLOTS).start()

        return carry

    gate = jnp.tanh(jnp.full((1, head_width), gate_ref[0], jnp.float32))
    ones = jnp.ones((HALVES * half_rows, head_width), jnp.bfloat16)

    def attend(h):
        for c in range(h * HALVES, (h + 1) * HALVES):
            for at in range(positions):
                share(c, at * 2 + 1 - core, 2, sibling).wait_recv()
        first = h * group * head_width

        def one_request(r, carry):
            span = pl.ds(pl.multiple_of(r * text_words, text_words), text_words)
            q = jnp.concatenate(
                [queries[span, first + g * head_width : first + (g + 1) * head_width] for g in range(group)], axis=0
            ).astype(jnp.bfloat16)
            total = jnp.zeros((group * text_words, wide), jnp.float32)
            for s in range(2):
                owner = slot_ref[ids_ref[r, s]]
                keys = keyval[h][owner, :, :head_width]
                values = keyval[h][owner, :, head_width:]
                scores = lax.dot_general(q, keys, (((1,), (1,)), ((), ())), preferred_element_type=jnp.float32)
                exponent = jnp.exp(scores).astype(jnp.bfloat16)
                total += jnp.dot(
                    exponent, jnp.concatenate([values, ones], axis=1), preferred_element_type=jnp.float32
                )
            result = gate * (total[:, :head_width] / total[:, head_width:])
            for g in range(group):
                attended[span, first + g * head_width : first + (g + 1) * head_width] = result[
                    g * text_words : (g + 1) * text_words
                ]
            return carry

        lax.fori_loop(0, requests, one_request, 0)

    ticks = chunks + positions - 1
    begun = 0
    for tick in range(ticks):
        for distance in range(positions - 1, 0, -1):
            if 0 <= tick - distance < chunks:
                pass_on(tick - distance, distance)
        if tick < chunks:
            finish_own(tick)
        if tick == chunks - 1:
            for d in range(1, feat_count):
                text_copy(d).wait_recv()
        if tick >= chunks - 1 and begun < pieces:
            until = pieces if tick >= min(chunks, ticks - 2) else pieces // 2
            lax.fori_loop(begun, until, project, 0)
            begun = until
        if tick == ticks - 2:
            for h in range(kv_local - 1):
                attend(h)
    attend(kv_local - 1)
    out_ref[...] = attended[...].astype(jnp.bfloat16)

    for c in range(chunks):
        for d in range(1, feat_count):
            partial_copy(c, d).wait_send()
        for at in range(positions):
            origin = at * 2 + core
            share(c, origin, 2, sibling).wait_send()

            @pl.when((position > 0) & (at >= position))
            def _():
                share(c, origin, 0, me_dp - 2).wait_send()

            @pl.when((position < positions - 1) & (at <= position))
            def _():
                share(c, origin, 1, me_dp + 2).wait_send()

    for d in range(1, feat_count):
        text_copy(d).wait_send()


def per_device(
    text_rows, q_weight, features, kv_weight, q_gain, k_gain, attn_gate, image_ids, image_slot
):
    rows, depth = text_rows.shape
    columns = q_weight.shape[1]
    head_width = q_gain.shape[0]
    wide = 2 * head_width
    feat_count, dp_count = lax.axis_size("feat"), lax.axis_size("dp")
    kv_local = kv_weight.shape[1] // wide // feat_count
    group = columns // (head_width * kv_local)
    tokens, width = features.shape[1:]
    half_rows = tokens // HALVES
    chunks = kv_local * HALVES
    smem = pl.BlockSpec(memory_space=pltpu.SMEM)
    vmem = pl.BlockSpec(memory_space=pltpu.VMEM)
    whole = pl.BlockSpec(memory_space=pl.ANY)
    dma = pltpu.SemaphoreType.DMA
    scratch = [
        pltpu.VMEM((HALVES, half_rows, width), jnp.bfloat16),
        pltpu.VMEM((feat_count, kv_local, width, wide), jnp.bfloat16),
        pltpu.VMEM((chunks, feat_count - 1, half_rows, wide), jnp.bfloat16),
        pltpu.VMEM((chunks, feat_count - 1, half_rows, wide), jnp.bfloat16),
        pltpu.VMEM((chunks, half_rows, wide), jnp.float32),
        pltpu.VMEM((feat_count, rows, depth), jnp.bfloat16),
        pltpu.VMEM((SLOTS, q_weight.shape[0], PIECE), jnp.bfloat16),
        pltpu.VMEM((rows, columns), jnp.float32),
        pltpu.VMEM((rows, columns), jnp.float32),
        dma((HALVES,)),
        dma((feat_count, kv_local)),
        dma((chunks, feat_count - 1)),
        dma((chunks, feat_count - 1)),
        dma((feat_count - 1,)),
        dma((feat_count - 1,)),
        dma((columns // PIECE,)),
        dma((3, chunks, dp_count)),
        dma((chunks, dp_count)),
    ] + [pltpu.VMEM((dp_count, tokens, wide), jnp.bfloat16) for _ in range(kv_local)]
    return pl.pallas_call(
        functools.partial(fused_kernel, (feat_count, dp_count, head_width, group, kv_local)),
        out_shape=jax.ShapeDtypeStruct((rows, columns), jnp.bfloat16),
        in_specs=[smem, smem, smem, vmem, whole, vmem, vmem, whole, whole],
        out_specs=vmem,
        scratch_shapes=scratch,
        compiler_params=pltpu.CompilerParams(
            collective_id=0, has_side_effects=True, vmem_limit_bytes=60 * MIB
        ),
        name="gated_cross_attention",
    )(
        image_ids, image_slot, attn_gate, text_rows, features[0],
        q_gain.reshape(1, -1), k_gain.reshape(1, -1), q_weight, kv_weight,
    )


def solution(mesh):
    in_specs = (
        P("dp", "feat"),
        P(None, "feat"),
        P("dp", None, "feat"),
        P("feat", None),
        P(),
        P(),
        P(),
        P("dp", None),
        P(),
    )
    out_specs = P("dp", "feat")
    return jax.shard_map(
        per_device, mesh=mesh, in_specs=in_specs, out_specs=out_specs, check_vma=False
    )
```

time: 318 us -> 127 us (0.40)
  waiting for transfers between devices: 188 us -> 0 us
  Pallas kernels: 0 us -> 122 us
  matrix products: 84 us -> 0 us
  local copies, waits for them, and re-layouts: 26.3 us -> 3.23 us
  between operations: 13.9 us -> 0.66 us
  other arithmetic: 4.23 us -> 0 us
    pallas_call x0 -> x1, Pallas kernels: none -> 122 us  [per_device(): pl.pallas_call(functools.partial(fused_kernel, (feat_count, dp_count, hea...]
    all_gather x2 -> x0, waiting for transfers between devices: 98.8 us -> none  [the longest x1 67.8 us: per_device(): shard_piece = lax.all_gather(keyval[None], 'dp', axis=0, tiled=True)]
    reduce_scatter x1 -> x0, waiting for transfers between devices: 88.5 us -> none  [per_device(): lax.psum_scatter(jnp.einsum('nf,fhc->hnc', vision_rows, weight_block, pre...]
    dot_general x18 -> x0, matrix products: 84 us -> none  [the longest x8 29.1 us: attend(): jnp.einsum('rhgd,hnd->rhgn', queries, keyval[..., :head_width], preferred...]
    reshape x2 -> x0, local copies, waits for them, and re-layouts: 11.7 us -> none  [the longest x1 10.7 us: per_device(): kv_table = kv_weight.reshape(kv_weight.shape[0], heads_all, 2 * head_width)]
    squeeze x8 -> x0, local copies, waits for them, and re-layouts: 10.4 us -> none  [add_one(): lax.dynamic_index_in_dim(shard_piece, position, 0, keepdims=False)]
  transfers between devices with their start and end apart: 3 -> 0, of which waited for: 3 -> 0; matrix products, arithmetic and copies ran while one was open for 7% -> 0% of each run, Pallas kernels for 0% -> 0%
where the time goes in v1:
time: 127 us; the launch traced here: 126 us
  Pallas kernels  122 us (96%)
  local copies, waits for them, and re-layouts  3.23 us (3%)
    pallas_call x1, Pallas kernels, per_device(): pl.pallas_call(functools.partial(fused_kernel, (feat_count, dp_count, hea...  122 us
    unnamed x2, local copies, waits for them, and re-layouts  3.23 us

profile of v1, /device:TPU:0, one launch (start us, length us, event | category | flops | bytes accessed | tf_op | source)
XLA Modules:
  0.0 125.9 jit_solution(15896330252851387256)
XLA Ops:
  0.7 1.4 %copy.10.ids_ref = s32[16,2]{1,0:T(8,128)} copy(s32[16,2]{0,1:T(2,128)} %param.16) | data formatting | bytes 256 | tf_op args[7]
  2.0 122.0 %gated_cross_attention.1 = bf16[128,2048]{1,0:T(8,128)(2,1)} custom-call(s32[16,2]{1,0:T(8,128)} %copy.10.ids_ref, s32[8]{0:T(128)} %slot_ref.1, f32[1]{0:T(128)S(6)} %copy.12.gate_ref, bf16[128,2048]{1,0:T(8,128)(2,1)} %text_ref.1, bf16[1024,1920]{1,0:T(8,128)(2,1)} %bitcast.3, f32[1,128]{1,0:T(1,128)} %bitcast.4, f32[1,128]{1,0:T(1,128)} %bitcast.5, ...), custom_call_target="tpu_custom_call" | custom-call | tf_op jit(solution)/shard_map/gated_cross_attention/pallas_call | solution.py:317
  124.0 1.9 %copy.13 = bf16[128,2048]{1,0:T(8,128)(2,1)} copy(bf16[128,2048]{1,0:T(8,128)(2,1)} %gated_cross_attention.1) | data formatting | bytes 1048576

commit v2 on v1

--- a/solution.py
+++ b/solution.py
@@ -10,8 +10,8 @@
 epsilon = 1e-05
 MIB = 1024 * 1024
 MESH = pl.DeviceIdType.MESH
-HALVES = 2
-SLOTS = 3
+HALVES = 4
+SLOTS = 4
 PIECE = 256
 
 
@@ -27,7 +27,7 @@
     sizes,
     ids_ref, slot_ref, gate_ref, text_ref, features_ref, q_gain_ref, k_gain_ref, q_weight_ref, kv_weight_ref,
     out_ref,
-    vision, kv_table, outgoing, incoming, own, text_full, weights, queries, attended,
+    vision, kv_table, outgoing, incoming, own, text_full, weights, queries, grouped, sums, attended,
     vision_sem, table_sem, rs_send, rs_recv, text_send, text_recv, weight_sem, kv_send, kv_recv,
     *keyval,
 ):
@@ -110,8 +110,7 @@
         )
 
     def share(c, origin, way, target):
-        h, half = c // HALVES, c % HALVES
-        block = keyval[h].at[origin, pl.ds(half * half_rows, half_rows), :]
+        block = keyval[c].at[origin]
         return pltpu.make_async_remote_copy(
             src_ref=block, dst_ref=block, send_sem=kv_send.at[way, c, origin],
             recv_sem=kv_recv.at[c, origin], device_id={"dp": target}, device_id_type=MESH,
@@ -136,19 +135,20 @@
         if half == 0:
             load_table(me_feat, h).wait()
         own[c] = jnp.dot(vision[half], kv_table[me_feat, h], preferred_element_type=jnp.float32)
-        if c == max(0, chunks - 2):
-            for d in range(1, feat_count):
+        for d in range(1, feat_count):
+            if c == min(chunks - 1, chunks // 4 + d - 1):
                 text_copy(d).start()
 
     def finish_own(c):
-        h, half = c // HALVES, c % HALVES
         summed = own[c]
         for d in range(1, feat_count):
             partial_copy(c, d).wait_recv()
             summed = summed + incoming[c, d - 1].astype(jnp.float32)
         normed_keys = head_norm(summed[:, :head_width], k_gain_ref[...])
-        block = jnp.concatenate([normed_keys, summed[:, head_width:]], axis=-1).astype(jnp.bfloat16)
-        keyval[h][me_dp, half * half_rows : (half + 1) * half_rows, :] = block
+        turned = jnp.concatenate(
+            [normed_keys[at : at + head_width].T for at in range(0, half_rows, head_width)], axis=0
+        )
+        keyval[c][me_dp] = jnp.concatenate([turned, summed[:, head_width:]], axis=-1).astype(jnp.bfloat16)
 
         @pl.when(position > 0)
         def _():
@@ -204,30 +204,46 @@
 
         return carry
 
-    gate = jnp.tanh(jnp.full((1, head_width), gate_ref[0], jnp.float32))
-    ones = jnp.ones((HALVES * half_rows, head_width), jnp.bfloat16)
-
-    def attend(h):
-        for c in range(h * HALVES, (h + 1) * HALVES):
-            for at in range(positions):
-                share(c, at * 2 + 1 - core, 2, sibling).wait_recv()
-        first = h * group * head_width
-
-        def one_request(r, carry):
-            span = pl.ds(pl.multiple_of(r * text_words, text_words), text_words)
-            q = jnp.concatenate(
+    def regroup(r, carry):
+        span = pl.ds(pl.multiple_of(r * text_words, text_words), text_words)
+        for h in range(kv_local):
+            first = h * group * head_width
+            grouped[h, r] = jnp.concatenate(
                 [queries[span, first + g * head_width : first + (g + 1) * head_width] for g in range(group)], axis=0
             ).astype(jnp.bfloat16)
-            total = jnp.zeros((group * text_words, wide), jnp.float32)
-            for s in range(2):
-                owner = slot_ref[ids_ref[r, s]]
-                keys = keyval[h][owner, :, :head_width]
-                values = keyval[h][owner, :, head_width:]
-                scores = lax.dot_general(q, keys, (((1,), (1,)), ((), ())), preferred_element_type=jnp.float32)
-                exponent = jnp.exp(scores).astype(jnp.bfloat16)
-                total += jnp.dot(
-                    exponent, jnp.concatenate([values, ones], axis=1), preferred_element_type=jnp.float32
-                )
+        return carry
+
+    gate = jnp.tanh(jnp.full((1, head_width), gate_ref[0], jnp.float32))
+    ones = jnp.ones((2 * half_rows, head_width), jnp.bfloat16)
+
+    def attend(c):
+        h, half = c // HALVES, c % HALVES
+        for at in range(positions):
+            share(c, at * 2 + 1 - core, 2, sibling).wait_recv()
+        first = h * group * head_width
+
+        def one_request(r, carry):
+            owners = [slot_ref[ids_ref[r, s]] for s in range(2)]
+            keys = jnp.concatenate(
+                [
+                    keyval[c][owner, at : at + head_width, :head_width]
+                    for owner in owners
+                    for at in range(0, half_rows, head_width)
+                ],
+                axis=1,
+            )
+            values = jnp.concatenate([keyval[c][owner, :, head_width:] for owner in owners], axis=0)
+            scores = jnp.dot(grouped[h, r], keys, preferred_element_type=jnp.float32)
+            exponent = jnp.exp(scores).astype(jnp.bfloat16)
+            total = jnp.dot(
+                exponent, jnp.concatenate([values, ones], axis=1), preferred_element_type=jnp.float32
+            )
+            if half > 0:
+                total += sums[r]
+            if half < HALVES - 1:
+                sums[r] = total
+                return carry
+            span = pl.ds(pl.multiple_of(r * text_words, text_words), text_words)
             result = gate * (total[:, :head_width] / total[:, head_width:])
             for g in range(group):
                 attended[span, first + g * head_width : first + (g + 1) * head_width] = result[
@@ -235,27 +251,33 @@
                 ]
             return carry
 
-        lax.fori_loop(0, requests, one_request, 0)
+        lax.fori_loop(0, requests, one_request, 0, unroll=2)
 
     ticks = chunks + positions - 1
-    begun = 0
+    begun = ready = 0
+    project_at = max(1, chunks - 3)
     for tick in range(ticks):
         for distance in range(positions - 1, 0, -1):
             if 0 <= tick - distance < chunks:
                 pass_on(tick - distance, distance)
         if tick < chunks:
             finish_own(tick)
-        if tick == chunks - 1:
+        if tick == project_at:
             for d in range(1, feat_count):
                 text_copy(d).wait_recv()
-        if tick >= chunks - 1 and begun < pieces:
-            until = pieces if tick >= min(chunks, ticks - 2) else pieces // 2
+        if tick >= project_at and begun < pieces:
+            until = min(pieces, begun + (pieces + 1) // 2)
             lax.fori_loop(begun, until, project, 0)
             begun = until
-        if tick == ticks - 2:
-            for h in range(kv_local - 1):
-                attend(h)
-    attend(kv_local - 1)
+            if begun == pieces:
+                lax.fori_loop(0, requests, regroup, 0)
+        elif begun == pieces:
+            for _ in range(2):
+                if ready <= tick - positions and ready < chunks:
+                    attend(ready)
+                    ready += 1
+    for c in range(ready, chunks):
+        attend(c)
     out_ref[...] = attended[...].astype(jnp.bfloat16)
 
     for c in range(chunks):
@@ -289,6 +311,7 @@
     group = columns // (head_width * kv_local)
     tokens, width = features.shape[1:]
     half_rows = tokens // HALVES
+    requests = image_ids.shape[0]
     chunks = kv_local * HALVES
     smem = pl.BlockSpec(memory_space=pltpu.SMEM)
     vmem = pl.BlockSpec(memory_space=pltpu.VMEM)
@@ -303,6 +326,8 @@
         pltpu.VMEM((feat_count, rows, depth), jnp.bfloat16),
         pltpu.VMEM((SLOTS, q_weight.shape[0], PIECE), jnp.bfloat16),
         pltpu.VMEM((rows, columns), jnp.float32),
+        pltpu.VMEM((kv_local, requests, group * rows // requests, head_width), jnp.bfloat16),
+        pltpu.VMEM((requests, group * rows // requests, wide), jnp.float32),
         pltpu.VMEM((rows, columns), jnp.float32),
         dma((HALVES,)),
         dma((feat_count, kv_local)),
@@ -313,7 +338,7 @@
         dma((columns // PIECE,)),
         dma((3, chunks, dp_count)),
         dma((chunks, dp_count)),
-    ] + [pltpu.VMEM((dp_count, tokens, wide), jnp.bfloat16) for _ in range(kv_local)]
+    ] + [pltpu.VMEM((dp_count, half_rows, wide), jnp.bfloat16) for _ in range(chunks)]
     return pl.pallas_call(
         functools.partial(fused_kernel, (feat_count, dp_count, head_width, group, kv_local)),
         out_shape=jax.ShapeDtypeStruct((rows, columns), jnp.bfloat16),

time: 127 us -> 116 us (0.913)
  Pallas kernels: 122 us -> 111 us
    pallas_call x1, Pallas kernels: 122 us -> 111 us  [per_device(): pl.pallas_call(functools.partial(fused_kernel, (feat_count, dp_count, hea...]
where the time goes in v2:
time: 116 us; the launch traced here: 115 us
  Pallas kernels  111 us (96%)
  local copies, waits for them, and re-layouts  3.23 us (3%)
    pallas_call x1, Pallas kernels, per_device(): pl.pallas_call(functools.partial(fused_kernel, (feat_count, dp_count, hea...  111 us
    unnamed x2, local copies, waits for them, and re-layouts  3.23 us

profile of v2, /device:TPU:0, one launch (start us, length us, event | category | flops | bytes accessed | tf_op | source)
XLA Modules:
  0.0 115.3 jit_solution(7421952954252804854)
XLA Ops:
  0.7 1.4 %copy.10.ids_ref = s32[16,2]{1,0:T(8,128)} copy(s32[16,2]{0,1:T(2,128)} %param.16) | data formatting | bytes 256 | tf_op args[7]
  2.0 111.4 %gated_cross_attention.1 = bf16[128,2048]{1,0:T(8,128)(2,1)} custom-call(s32[16,2]{1,0:T(8,128)} %copy.10.ids_ref, s32[8]{0:T(128)} %slot_ref.1, f32[1]{0:T(128)S(6)} %copy.12.gate_ref, bf16[128,2048]{1,0:T(8,128)(2,1)} %text_ref.1, bf16[1024,1920]{1,0:T(8,128)(2,1)} %bitcast.3, f32[1,128]{1,0:T(1,128)} %bitcast.4, f32[1,128]{1,0:T(1,128)} %bitcast.5, ...), custom_call_target="tpu_custom_call" | custom-call | tf_op jit(solution)/shard_map/gated_cross_attention/pallas_call | solution.py:342
  113.4 1.9 %copy.13 = bf16[128,2048]{1,0:T(8,128)(2,1)} copy(bf16[128,2048]{1,0:T(8,128)(2,1)} %gated_cross_attention.1) | data formatting | bytes 1048576

commit v3 on v2

--- a/solution.py
+++ b/solution.py
@@ -11,8 +11,9 @@
 MIB = 1024 * 1024
 MESH = pl.DeviceIdType.MESH
 HALVES = 4
-SLOTS = 4
-PIECE = 256
+SLOTS = 8
+PIECE = 512
+LEAD = 4
 
 
 def head_norm(values, gain_vector):
@@ -38,7 +39,8 @@
     wide = 2 * head_width
     half_rows = vision.shape[1]
     chunks = kv_local * HALVES
-    pieces = q_weight_ref.shape[1] // PIECE
+    across = q_weight_ref.shape[1] // PIECE
+    pieces = feat_count * across
     depth = text_ref.shape[1]
     positions = dp_count // 2
     me_feat, me_dp = lax.axis_index("feat"), lax.axis_index("dp")
@@ -57,9 +59,11 @@
         )
 
     def load_weight(j):
-        start = pl.multiple_of(j * PIECE, PIECE)
+        source = (me_feat - j // across + feat_count) % feat_count
+        down = pl.multiple_of(source * depth, depth)
+        start = pl.multiple_of(j % across * PIECE, PIECE)
         return pltpu.make_async_copy(
-            q_weight_ref.at[:, pl.ds(start, PIECE)], weights.at[j % SLOTS], weight_sem.at[j]
+            q_weight_ref.at[pl.ds(down, depth), pl.ds(start, PIECE)], weights.at[j % SLOTS], weight_sem.at[j]
         )
 
     load_vision(0).start()
@@ -116,12 +120,12 @@
             recv_sem=kv_recv.at[c, origin], device_id={"dp": target}, device_id_type=MESH,
         )
 
-    for c in range(chunks):
+    def project_piece(c):
         h, half = c // HALVES, c % HALVES
         if h == 0:
             load_vision(half).wait()
 
-        def one_peer(d, carry, c=c, h=h, half=half):
+        def one_peer(d, carry):
             f = (me_feat + d) % feat_count
             if half == 0:
                 load_table(f, h).wait()
@@ -136,7 +140,7 @@
             load_table(me_feat, h).wait()
         own[c] = jnp.dot(vision[half], kv_table[me_feat, h], preferred_element_type=jnp.float32)
         for d in range(1, feat_count):
-            if c == min(chunks - 1, chunks // 4 + d - 1):
+            if c == min(chunks - 1, chunks // 2 - 2 + d):
                 text_copy(d).start()
 
     def finish_own(c):
@@ -185,24 +189,22 @@
 
     def project(j, carry):
         load_weight(j).wait()
-        total = jnp.zeros((rows, PIECE), jnp.float32)
-        for f in range(feat_count):
-            total += jnp.dot(
-                text_full[f],
-                weights[j % SLOTS, f * depth : (f + 1) * depth, :],
-                preferred_element_type=jnp.float32,
-            )
-        for part in range(PIECE // head_width):
-            normed = head_norm(total[:, part * head_width : (part + 1) * head_width], q_gain_ref[...])
-            normed = (normed * head_width ** (-0.5)).astype(jnp.bfloat16)
-            start = pl.multiple_of(j * PIECE + part * head_width, head_width)
-            queries[:, pl.ds(start, head_width)] = normed.astype(jnp.float32)
+        source = (me_feat - j // across + feat_count) % feat_count
+        columns = pl.ds(pl.multiple_of(j % across * PIECE, PIECE), PIECE)
+        queries[:, columns] += jnp.dot(
+            text_full[source], weights[j % SLOTS], preferred_element_type=jnp.float32
+        )
 
         @pl.when(j + SLOTS < pieces)
         def _():
             load_weight(j + SLOTS).start()
 
         return carry
+
+    def norm_queries():
+        for at in range(0, queries.shape[1], head_width):
+            normed = head_norm(queries[:, at : at + head_width], q_gain_ref[...])
+            queries[:, at : at + head_width] = normed * head_width ** (-0.5)
 
     def regroup(r, carry):
         span = pl.ds(pl.multiple_of(r * text_words, text_words), text_words)
@@ -254,24 +256,29 @@
         lax.fori_loop(0, requests, one_request, 0, unroll=2)
 
     ticks = chunks + positions - 1
-    begun = ready = 0
-    project_at = max(1, chunks - 3)
-    for tick in range(ticks):
+    ready = 0
+    queries[...] = jnp.zeros_like(queries)
+    project_piece(0)
+    for step in range(1, ticks + LEAD):
+        if step < chunks:
+            project_piece(step)
+        tick = step - LEAD
+        if tick < 0:
+            continue
         for distance in range(positions - 1, 0, -1):
             if 0 <= tick - distance < chunks:
                 pass_on(tick - distance, distance)
         if tick < chunks:
             finish_own(tick)
-        if tick == project_at:
-            for d in range(1, feat_count):
+        due = [d for d in range(feat_count) if min(chunks // 2 - 1 + d if d else 0, ticks - 2) == tick]
+        for d in due:
+            if d > 0:
                 text_copy(d).wait_recv()
-        if tick >= project_at and begun < pieces:
-            until = min(pieces, begun + (pieces + 1) // 2)
-            lax.fori_loop(begun, until, project, 0)
-            begun = until
-            if begun == pieces:
-                lax.fori_loop(0, requests, regroup, 0)
-        elif begun == pieces:
+            lax.fori_loop(d * across, (d + 1) * across, project, 0)
+        if feat_count - 1 in due:
+            norm_queries()
+            lax.fori_loop(0, requests, regroup, 0)
+        elif tick > min(chunks // 2 + feat_count - 2, ticks - 2):
             for _ in range(2):
                 if ready <= tick - positions and ready < chunks:
                     attend(ready)
@@ -324,7 +331,7 @@
         pltpu.VMEM((chunks, feat_count - 1, half_rows, wide), jnp.bfloat16),
         pltpu.VMEM((chunks, half_rows, wide), jnp.float32),
         pltpu.VMEM((feat_count, rows, depth), jnp.bfloat16),
-        pltpu.VMEM((SLOTS, q_weight.shape[0], PIECE), jnp.bfloat16),
+        pltpu.VMEM((SLOTS, depth, PIECE), jnp.bfloat16),
         pltpu.VMEM((rows, columns), jnp.float32),
         pltpu.VMEM((kv_local, requests, group * rows // requests, head_width), jnp.bfloat16),
         pltpu.VMEM((requests, group * rows // requests, wide), jnp.float32),
@@ -335,7 +342,7 @@
         dma((chunks, feat_count - 1)),
         dma((feat_count - 1,)),
         dma((feat_count - 1,)),
-        dma((columns // PIECE,)),
+        dma((feat_count * columns // PIECE,)),
         dma((3, chunks, dp_count)),
         dma((chunks, dp_count)),
     ] + [pltpu.VMEM((dp_count, half_rows, wide), jnp.bfloat16) for _ in range(chunks)]

time: 116 us -> 116 us (level)
  no operation moved by 1% of the time
where the time goes in v3:
time: 116 us; the launch traced here: 115 us
  Pallas kernels  112 us (97%)
  local copies, waits for them, and re-layouts  3.23 us (3%)
    pallas_call x1, Pallas kernels, per_device(): pl.pallas_call(functools.partial(fused_kernel, (feat_count, dp_count, hea...  112 us
    unnamed x2, local copies, waits for them, and re-layouts  3.23 us

profile of v3, /device:TPU:0, one launch (start us, length us, event | category | flops | bytes accessed | tf_op | source)
XLA Modules:
  0.0 115.4 jit_solution(520755359081966143)
XLA Ops:
  0.7 1.4 %copy.10.ids_ref = s32[16,2]{1,0:T(8,128)} copy(s32[16,2]{0,1:T(2,128)} %param.16) | data formatting | bytes 256 | tf_op args[7]
  2.0 111.5 %gated_cross_attention.1 = bf16[128,2048]{1,0:T(8,128)(2,1)} custom-call(s32[16,2]{1,0:T(8,128)} %copy.10.ids_ref, s32[8]{0:T(128)} %slot_ref.1, f32[1]{0:T(128)S(6)} %copy.12.gate_ref, bf16[128,2048]{1,0:T(8,128)(2,1)} %text_ref.1, bf16[1024,1920]{1,0:T(8,128)(2,1)} %bitcast.3, f32[1,128]{1,0:T(1,128)} %bitcast.4, f32[1,128]{1,0:T(1,128)} %bitcast.5, ...), custom_call_target="tpu_custom_call" | custom-call | tf_op jit(solution)/shard_map/gated_cross_attention/pallas_call | solution.py:349
  113.5 1.9 %copy.13 = bf16[128,2048]{1,0:T(8,128)(2,1)} copy(bf16[128,2048]{1,0:T(8,128)(2,1)} %gated_cross_attention.1) | data formatting | bytes 1048576
